TPU v7x, 256 devices: a whole 4x4x8 slice. The times are simulated.
256 devices in a mesh: group: 8 (over x_hi, y), seq: 32 (over z, x_lo, core).
Axes of the slice: x: 4 (x_hi: 2, x_lo: 2; x = x_hi * 2 + x_lo), y: 4, z: 8, core: 2. Of those that a mesh axis runs over, the one named last changes fastest.
Arguments:
- queries: bfloat16 [8, 4096, 4096], P('group', 'seq'), may hold values from -100 to 100
- current_kv: bfloat16 [8, 4096, 2, 4096], P('group', 'seq'), may hold values from -5 to 5
- text_kv: bfloat16 [8, 256, 2, 4096], P('group', 'seq'), may hold values from -5 to 5
- cache_kv: bfloat16 [32, 512, 2, 4096], P('group', 'seq'), may hold values from -6 to 6
- window_ids: int32 [8, 4], replicated, may hold values from 0 to 31, as said below
- window_count: int32 [8], replicated, may hold values from 1 to 4, as said below
- cache_slot: int32 [32], replicated, may hold values from 0 to 31, as said below
- text_count: int32 [8], replicated, may hold values from 2 to 256, as said below
Outputs:
- attended: float32 [8, 4096, 4096], P('group', 'seq')
Inputs may be any that keep to these rules, and one draw needn't show every extreme that they name: `window_ids`: each row names 4 different cached clips; their slots lie on exactly two indices of group (slot // 4), 2 on each. Only the first window_count[g] entries of row g are live; some clip has all 4 live and another clip only one. A permutation: cached clip c lies in slot cache_slot[c]. `text_count`: some clip uses all 256 caption tokens and another clip only two.
All inputs are finite; a program needn't handle non-finite values.
Results may differ from a plain program's by a relative error of at most 0.0013.
Values may be sent and summed in bfloat16 or wider, within the bound.
A program may use at most 64 MiB of HBM per device.

v0:
```python
import math

import jax
import jax.numpy as jnp
from jax import lax
from jax.sharding import PartitionSpec as P

HEAD = 128
WINDOW = 4


def attend(query_rows, key_rows, value_rows, live_mask):
    scores = jnp.dot(query_rows, key_rows.T, preferred_element_type=jnp.float32) * (
        1.0 / math.sqrt(query_rows.shape[1])
    )
    scores = jnp.where(live_mask[None, :], scores, -1e30)
    row_max = jnp.max(scores, axis=1, keepdims=True)
    weights = jnp.exp(scores - row_max)
    row_sum = jnp.sum(weights, axis=1, keepdims=True)
    weighted = jnp.dot(weights.astype(jnp.bfloat16), value_rows, preferred_element_type=jnp.float32)
    return weighted / row_sum


def on_device(
    queries, current_kv, text_kv, cache_kv, window_ids, window_count, cache_slot, text_count
):
    tok_rows = queries.shape[1]
    full_width = queries.shape[2]
    seq_count = lax.axis_size("seq")
    local_width = full_width // seq_count
    local_heads = local_width // HEAD
    my_clip = lax.axis_index("group")
    query_cols = queries.reshape(tok_rows, 1, full_width)
    current_cols = current_kv.reshape(tok_rows, 2, full_width)
    text_cols = text_kv.reshape(text_kv.shape[1], 2, full_width)
    query_all, current_all, text_all = (
        lax.all_to_all(query_cols, "seq", split_axis=2, concat_axis=0, tiled=True),
        lax.all_to_all(current_cols, "seq", split_axis=2, concat_axis=0, tiled=True),
        lax.all_to_all(text_cols, "seq", split_axis=2, concat_axis=0, tiled=True),
    )
    slot_table = cache_slot[window_ids]
    pool_rows = lax.all_gather(cache_kv, "group", axis=0, tiled=True)
    picked = jnp.take(pool_rows, slot_table[my_clip], axis=0)
    picked = lax.all_to_all(picked, "seq", split_axis=3, concat_axis=1, tiled=True)
    cache_tok = picked.shape[1]
    cache_span = WINDOW * cache_tok
    key_rows = jnp.concatenate(
        [current_all[:, 0], picked[:, :, 0].reshape(cache_span, local_width)], axis=0
    )
    value_rows = jnp.concatenate(
        [current_all[:, 1], picked[:, :, 1].reshape(cache_span, local_width)], axis=0
    )
    clip_rows = query_all.shape[0]
    live_mask = jnp.concatenate(
        [
            jnp.ones((clip_rows,), bool),
            jnp.arange(cache_span, dtype=jnp.int32) // cache_tok < window_count[my_clip],
        ]
    )
    text_live = jnp.arange(text_all.shape[0], dtype=jnp.int32) < text_count[my_clip]
    query_flat = query_all[:, 0]
    text_keys = text_all[:, 0]
    text_values = text_all[:, 1]
    block_rows = math.gcd(512, clip_rows)

    def per_head(head_index):
        query_blocks = query_flat.reshape(clip_rows // block_rows, block_rows, HEAD)

        def per_block(query_rows):
            return attend(query_rows, key_rows, value_rows, live_mask) + attend(
                query_rows, text_keys, text_values, text_live
            )

        return lax.map(per_block, query_blocks).reshape(clip_rows, HEAD)

    head_out = lax.map(per_head, jnp.arange(local_heads, dtype=jnp.int32))
    merged = head_out.transpose(1, 0, 2).reshape(clip_rows, local_width)
    tokens_back = lax.all_to_all(merged, "seq", split_axis=0, concat_axis=1, tiled=True)
    return tokens_back.reshape(1, tok_rows, full_width)


def solution(mesh):
    return jax.shard_map(
        on_device,
        mesh=mesh,
        in_specs=(
            P("group", "seq", None),
            P("group", "seq", None, None),
            P("group", "seq", None, None),
            P("group", "seq", None, None),
            P(),
            P(),
            P(),
            P(),
        ),
        out_specs=P("group", "seq", None),
        check_vma=False,
    )
```

profile of v0, /device:TPU:1, one launch (start us, length us, event | category | flops | bytes accessed | tf_op | source)
XLA Modules:
  0.0 390.7 jit_solution(6723075100806749187)
XLA Ops:
  6.5 2.9 copy.58
  9.5 3.8 copy.62
  13.3 3.3 bitcast_bitcast_fusion
  16.7 2.9 reshape.88
  19.5 11.0 %all-to-all-start.3 = ((bf16[32,2,1024]{2,1,0:T(2,128)(2,1)}), bf16[32,2,1024]{2,1,0:T(2,128)(2,1)S(1)}, u32[]{:S(2)}, u32[]{:S(2)}) async-start(bf16[32,2,1024]{2,1,0:T(2,128)(2,1)} %reshape.88), calls=%async_computation.3 | async-start | bytes 262144 | tf_op jit(solution)/shard_map/all_to_all | solution.py:39
  34.0 22.4 %reduce = bf16[4096,128]{1,0:T(8,128)(2,1)S(1)} reduce(bf16[4096,1,128]{2,1,0:T(2,128)(2,1)S(1)} %bitcast.87, bf16[]{:T(256)} %broadcast.75), dimensions={1}, to_apply=%bitcast.51.reduce_sub_computation | reduce | bytes 2097154
  57.5 8.4 %all-to-all-start = ((bf16[32,2,8192]{2,1,0:T(2,128)(2,1)}), bf16[32,2,8192]{2,1,0:T(2,128)(2,1)S(1)}, u32[]{:S(2)}, u32[]{:S(2)}) async-start(bf16[32,2,8192]{2,1,0:T(2,128)(2,1)} %reshape.84), calls=%async_computation | async-start | bytes 2097152 | tf_op jit(solution)/shard_map/all_to_all | solution.py:37
  65.9 5.6 %copy.55 = bf16[1,128,2,4096]{1,2,3,0:T(2,128)(2,1)} copy(bf16[1,128,2,4096]{3,2,1,0:T(2,128)(2,1)S(1)} %copy-done.6) | data formatting | bytes 4194304 | tf_op args[1]
  71.6 22.5 %all-to-all-done = bf16[32,2,8192]{2,1,0:T(2,128)(2,1)S(1)} async-done(((bf16[32,2,8192]{2,1,0:T(2,128)(2,1)}), bf16[32,2,8192]{2,1,0:T(2,128)(2,1)S(1)}, u32[]{:S(2)}, u32[]{:S(2)}) %all-to-all-start) | async-done | bytes 1048608 | tf_op jit(solution)/shard_map/all_to_all | solution.py:37
  95.0 4.9 %all-to-all-start.1 = ((bf16[128,2,4096]{0,1,2:T(2,128)(2,1)}), bf16[128,2,4096]{0,1,2:T(2,128)(2,1)S(1)}, u32[]{:S(2)}, u32[]{:S(2)}) async-start(bf16[128,2,4096]{0,1,2:T(2,128)(2,1)} %bitcast.85), calls=%async_computation.1 | async-start | bytes 4194304 | tf_op jit(solution)/shard_map/all_to_all | solution.py:38
  101.0 59.0 %all-gather.2.cloned.1.call-done = bf16[32,16,2,4096]{3,1,2,0:T(8,128)(2,1)} async-done(((bf16[4,16,2,4096]{3,1,2,0:T(8,128)(2,1)}), bf16[32,16,2,4096]{3,1,2,0:T(8,128)(2,1)}) %all-gather.2.cloned.1.call-update) | async-done | bytes 8388624 | tf_op jit(solution)/shard_map/all_gather | solution.py:42
  160.0 5.1 %gather_fusion.1 = bf16[4,16,2,4096]{3,1,2,0:T(8,128)(2,1)} fusion(bf16[32,16,2,4096]{3,1,2,0:T(8,128)(2,1)} %all-gather.2.cloned.1.call-done, s32[1024]{0:T(1024)S(1)} %pad_clamp_fusion), kind=kCustom, calls=%fused_computation.1 | custom fusion | bytes 2097168 | tf_op jit(solution)/shard_map/jit(_take)/gather | solution.py:43
  166.4 8.8 %copy.59 = bf16[4,16,2,4096]{1,0,2,3:T(4,128)(2,1)} copy(bf16[4,16,2,4096]{3,1,2,0:T(8,128)(2,1)S(1)} %broadcast_select_fusion) | data formatting | bytes 2097152 | tf_op jit(solution)/shard_map/jit(_take)/select_n | solution.py:43
  175.2 11.2 %reshape.86 = bf16[32,2,8192]{2,1,0:T(2,128)(2,1)} reshape(bf16[4096,2,4,16]{3,2,1,0:T(4,128)(2,1)} %bitcast.81) | data formatting | bytes 2097152
  186.4 9.3 %all-to-all-start.2 = ((bf16[32,2,8192]{2,1,0:T(2,128)(2,1)}), bf16[32,2,8192]{2,1,0:T(2,128)(2,1)}, u32[]{:S(2)}, u32[]{:S(2)}) async-start(bf16[32,2,8192]{2,1,0:T(2,128)(2,1)} %reshape.86), calls=%async_computation.2 | async-start | bytes 2097152 | tf_op jit(solution)/shard_map/all_to_all | solution.py:44
  197.7 3.5 reshape.89
  201.2 4.5 %copy.63 = bf16[32,8,2,128]{3,1,0,2:T(8,128)(2,1)S(1)} copy(bf16[32,8,2,128]{1,2,3,0:T(2,128)(2,1)} %bitcast.88) | data formatting | bytes 262144 | tf_op jit(solution)/shard_map/all_to_all | solution.py:39
  209.8 3.8 copy.56
  213.6 3.0 slice_bitcast_fusion
  216.6 7.3 %all-to-all-done.2 = bf16[32,2,8192]{2,1,0:T(2,128)(2,1)} async-done(((bf16[32,2,8192]{2,1,0:T(2,128)(2,1)}), bf16[32,2,8192]{2,1,0:T(2,128)(2,1)}, u32[]{:S(2)}, u32[]{:S(2)}) %all-to-all-start.2) | async-done | bytes 1048608 | tf_op jit(solution)/shard_map/all_to_all | solution.py:44
  223.9 8.9 %reshape.87 = bf16[4096,2,4,16]{3,2,1,0:T(4,128)(2,1)} reshape(bf16[32,2,8192]{2,1,0:T(2,128)(2,1)} %all-to-all-done.2) | data formatting | bytes 2097152
  232.9 10.3 %copy.67 = bf16[4,16,2,32,128]{4,1,3,2,0:T(8,128)(2,1)S(1)} copy(bf16[4,16,2,32,128]{1,0,2,4,3:T(4,128)(2,1)} %bitcast.82) | data formatting | bytes 2097152 | tf_op jit(solution)/shard_map/all_to_all | solution.py:44
  243.2 3.0 pad_maximum_fusion
  246.2 77.4 %while.18 = (s32[]{:T(128)}, f32[8,512,128]{2,1,0:T(8,128)}, pred[6144]{0:T(1024)(128)(4,1)S(1)}, bf16[8,512,128]{2,1,0:T(8,128)(2,1)S(1)}, bf16[6144,128]{1,0:T...) while((s32[]{:T(128)}, f32[8,512,128]{2,1,0:T(8,128)}, ...), condition=%wide.region_5.6_spmd.clone, body=%wide.region_0.5_spmd.clone.sunk | while | flops 1713436928 | bytes 49978764 | solution.py:74
  248.4 2.9 fusion.58
  277.4 2.9 fusion.58
  287.1 2.9 fusion.58
  296.7 2.9 fusion.58
  306.4 2.9 fusion.58
  316.1 2.9 fusion.58
  323.6 55.5 %all_to_all.85 = f32[32,128,128]{2,1,0:T(8,128)S(1)} all-to-all(f32[32,128,128]{2,1,0:T(8,128)} %bitcast.27), channel_id=1, replica_groups=mesh['group'=8,'seq'=32] {'seq'}, dimensions={0} | all-to-all | bytes 4194304 | tf_op jit(solution)/shard_map/all_to_all | solution.py:78
  380.9 2.9 copy.65
  (118 shorter events, 75.8 us)
Async XLA Ops:
  6.5 93.6 %copy-start = (s32[32]{0:T(128)S(1)}, s32[32]{0:T(128)}, u32[]{:S(2)}) copy-start(s32[32]{0:T(128)} %param.16) | copy-start | bytes 388
  6.5 2.9 copy-start.9
  6.5 153.4 %all-gather.2.cloned.1.call-start = ((), (), s32[]{:S(2)}) async-start(), calls=%async_computation.5 | async-start | bytes 9437184 | tf_op jit(solution)/shard_map/all_gather | solution.py:42
  13.3 17.3 %copy-start.8 = (bf16[1,128,4096]{2,1,0:T(8,128)(2,1)S(1)}, bf16[1,128,4096]{2,1,0:T(8,128)(2,1)}, u32[]{:S(2)}) copy-start(bf16[1,128,4096]{2,1,0:T(8,128)(2,1)} %param.10) | copy-start | bytes 3145732
  19.5 38.0 %all-to-all-start.3 = ((bf16[32,2,1024]{2,1,0:T(2,128)(2,1)}), bf16[32,2,1024]{2,1,0:T(2,128)(2,1)S(1)}, u32[]{:S(2)}, u32[]{:S(2)}) async-start(bf16[32,2,1024]{2,1,0:T(2,128)(2,1)} %reshape.88), calls=%async_computation.3 | async-start | bytes 262144 | tf_op jit(solution)/shard_map/all_to_all | solution.py:39
  57.5 8.4 %copy-start.6 = (bf16[1,128,2,4096]{3,2,1,0:T(2,128)(2,1)S(1)}, bf16[1,128,2,4096]{3,2,1,0:T(2,128)(2,1)}, u32[]{:S(2)}) copy-start(bf16[1,128,2,4096]{3,2,1,0:T(2,128)(2,1)} %param.11) | copy-start | bytes 6291460
  57.5 36.6 %all-to-all-start = ((bf16[32,2,8192]{2,1,0:T(2,128)(2,1)}), bf16[32,2,8192]{2,1,0:T(2,128)(2,1)S(1)}, u32[]{:S(2)}, u32[]{:S(2)}) async-start(bf16[32,2,8192]{2,1,0:T(2,128)(2,1)} %reshape.84), calls=%async_computation | async-start | bytes 2097152 | tf_op jit(solution)/shard_map/all_to_all | solution.py:37
  71.6 28.4 %copy-start.10 = (s32[8,4]{0,1:T(4,128)S(1)}, s32[8,4]{0,1:T(4,128)}, u32[]{:S(2)}) copy-start(s32[8,4]{0,1:T(4,128)} %param.14) | copy-start | bytes 388
  94.1 1.0 copy-start.4
  95.0 91.4 %all-to-all-start.1 = ((bf16[128,2,4096]{0,1,2:T(2,128)(2,1)}), bf16[128,2,4096]{0,1,2:T(2,128)(2,1)S(1)}, u32[]{:S(2)}, u32[]{:S(2)}) async-start(bf16[128,2,4096]{0,1,2:T(2,128)(2,1)} %bitcast.85), calls=%async_computation.1 | async-start | bytes 4194304 | tf_op jit(solution)/shard_map/all_to_all | solution.py:38
  175.2 20.6 %copy-start.11 = (s32[8]{0:T(128)S(1)}, s32[8]{0:T(128)}, u32[]{:S(2)}) copy-start(s32[8]{0:T(128)} %param.15) | copy-start | bytes 100
  175.2 21.2 %copy-start.12 = (s32[8]{0:T(128)S(1)}, s32[8]{0:T(128)}, u32[]{:S(2)}) copy-start(s32[8]{0:T(128)} %param.17) | copy-start | bytes 100
  186.4 19.3 %copy-start.5 = (bf16[32,2,8192]{2,1,0:T(2,128)(2,1)S(1)}, bf16[32,2,8192]{2,1,0:T(2,128)(2,1)}, u32[]{:S(2)}) copy-start(bf16[32,2,8192]{2,1,0:T(2,128)(2,1)} %copy-done.4) | copy-start | bytes 3145732
  186.4 19.3 %copy-start.2 = (bf16[128,2,4096]{0,1,2:T(2,128)(2,1)}, bf16[128,2,4096]{0,1,2:T(2,128)(2,1)S(1)}, u32[]{:S(2)}) copy-start(bf16[128,2,4096]{0,1,2:T(2,128)(2,1)S(1)} %all-to-all-done.1) | copy-start | bytes 6291460
  186.4 37.5 %all-to-all-start.2 = ((bf16[32,2,8192]{2,1,0:T(2,128)(2,1)}), bf16[32,2,8192]{2,1,0:T(2,128)(2,1)}, u32[]{:S(2)}, u32[]{:S(2)}) async-start(bf16[32,2,8192]{2,1,0:T(2,128)(2,1)} %reshape.86), calls=%async_computation.2 | async-start | bytes 2097152 | tf_op jit(solution)/shard_map/all_to_all | solution.py:44
  207.9 1.9 copy-start.3
  248.4 2.9 copy-start.7
  258.0 2.9 copy-start.7
  267.7 2.9 copy-start.7
  277.4 2.9 copy-start.7
  287.1 2.9 copy-start.7
  296.7 2.9 copy-start.7
  306.4 2.9 copy-start.7
  316.1 2.9 copy-start.7
  379.1 4.7 %copy-start.1 = (s32[32]{0:T(128)S(1)}, s32[32]{0:T(128)}, u32[]{:S(2)}) copy-start(s32[32]{0:T(128)} %param.16) | copy-start | bytes 388
Sparse Core Ops, SparseCore 0:
  10.0 149.9 all-gather.1
where the time goes:
time: 392 us; the launch traced here: 391 us
  local copies, waits for them, and re-layouts  94.3 us (24%)
  waiting for transfers between devices  88.8 us (23%)
  other arithmetic  56.9 us (15%)
  blocking collectives  55.5 us (14%)
  matrix products  47.7 us (12%)
  starting transfers between devices  33.6 us (9%)
  between operations  13.6 us (3%)
    all_gather x1, waiting for transfers between devices, on_device(): pool_rows = lax.all_gather(cache_kv, 'group', axis=0, tiled=True)  59 us
    all_to_all x1, blocking collectives, on_device(): lax.all_to_all(merged, 'seq', split_axis=0, concat_axis=1, tiled=True)  55.5 us
    unnamed x36, local copies, waits for them, and re-layouts  47.2 us
    dot_general x16, matrix products, attend(): jnp.dot(weights.astype(jnp.bfloat16), value_rows, preferred_element_type=...  28.6 us
    reduce_sum x16, other arithmetic, attend(): row_sum = jnp.sum(weights, axis=1, keepdims=True)  23.9 us
    all_to_all x1, waiting for transfers between devices, on_device(): lax.all_to_all(query_cols, 'seq', split_axis=2, concat_axis=0, tiled=True)  22.5 us
    unnamed x1, other arithmetic  22.4 us
    dot_general x16, matrix products, attend(): jnp.dot(query_rows, key_rows.T, preferred_element_type=jnp.float32)  19.1 us
  transfers between devices with their start and end apart: 5, of which 3 were waited for; matrix products, arithmetic and copies ran while one was open for 23% of the time, Pallas kernels for 0%

commit v1 on v0

v1 whole, which is shorter than its diff:
```python
import math

import jax
import jax.numpy as jnp
from jax import lax
from jax.experimental import pallas as pl
from jax.experimental.pallas import tpu as pltpu
from jax.sharding import PartitionSpec as P

HEAD = 128
WINDOW = 4
OWN = 4
NZ, NY = 8, 4
SEQ = 32
TOK = 128
KEYS = SEQ * TOK
CTOK = 16
CACHE = SEQ * CTOK
TTOK = 8
TEXT = SEQ * TTOK
ROWS = 512
CHUNKS = KEYS // ROWS
TILE = 512
SPAN = KEYS + WINDOW * CACHE
PARTS = 4
PART = CACHE // PARTS
SELF = 28
DEAD = -1e30
EXP_SCALE = math.log2(math.e) / math.sqrt(HEAD)
SEND_SCALE = 2.0**28
MESH = pl.DeviceIdType.MESH
BF16 = jnp.bfloat16
F32 = jnp.float32


def split_matrix(rows):
    half = rows // 2
    to = lax.broadcasted_iota(jnp.int32, (rows, rows), 0)
    at = lax.broadcasted_iota(jnp.int32, (rows, rows), 1)
    return jnp.where(at == jnp.where(to < half, 2 * to, 2 * to - rows + 1), 1.0, 0.0).astype(BF16)


def split_rows(matrix, mixed):
    return jnp.dot(matrix, mixed, preferred_element_type=F32).astype(BF16)


def body(
    q_hbm, kv_hbm, text_hbm, cache_hbm, ids, counts, slots, text_counts,
    out_hbm,
    q_raw, kv_raw, text_raw, cache_raw,
    kv_stage, cache_stage,
    q_buf, kv_buf, text_buf, text_kv,
    pool_0, pool_1, pool_2, pool_3,
    give_0, give_1, give_2, give_3,
    got_0, got_1, got_2, got_3,
    window, scores, o_buf,
    load_sem, send_sem, send_y, send_x, recv_sem, recv_q, recv_c, recv_y, recv_x,
):
    pools = (pool_0, pool_1, pool_2, pool_3)
    gives = (give_0, give_1, give_2, give_3)
    gots = (got_0, got_1, got_2, got_3)
    group = lax.axis_index("group")
    seq = lax.axis_index("seq")
    x_hi, y = group // NY, group % NY
    z, x_lo, core = seq // 4, (seq // 2) % 2, seq % 2

    def head_of(z_at, x_at, core_at):
        return z_at * 4 + ((x_at + x_hi) % 2) * 2 + core_at

    def place(step, sign):
        n = (step // 4 + 1) % NZ
        shift = (2 * (n % 2) - 1) * ((n + 1) // 2) * sign
        return (z + shift + NZ) % NZ, (x_lo + (step % 4) // 2) % 2, (core + step % 2) % 2

    def target(step, sign=1):
        z_at, x_at, core_at = place(step, sign)
        return (group, z_at * 4 + x_at * 2 + core_at)

    def columns(step):
        return pl.ds(pl.multiple_of(head_of(*place(step, 1)) * HEAD, HEAD), HEAD)

    def y_target(shift):
        return (x_hi * NY + (y + shift) % NY, seq)

    x_target = ((1 - x_hi) * NY + y, z * 4 + (1 - x_lo) * 2 + core)

    def push(src, dst, send, recv, device):
        pltpu.make_async_remote_copy(
            src_ref=src, dst_ref=dst, send_sem=send, recv_sem=recv, device_id=device, device_id_type=MESH
        ).start()

    def await_bytes(ref, sem):
        pltpu.make_async_copy(ref, ref, sem).wait()

    def each(lo, hi, fn):
        def run(step, carry):
            fn(step)
            return carry

        lax.fori_loop(lo, hi, run, 0)

    def each_remote(fn):
        each(0, SELF, fn)
        each(SELF + 1, SEQ, fn)

    loads = [
        pltpu.make_async_copy(src, dst, load_sem.at[i])
        for i, (src, dst) in enumerate(
            ((cache_hbm, cache_raw), (kv_hbm, kv_raw), (text_hbm, text_raw), (q_hbm, q_raw))
        )
    ]
    for load in loads:
        load.start()

    barrier = pltpu.get_barrier_semaphore()

    def greet(device):
        pl.semaphore_signal(barrier, inc=1, device_id=device, device_id_type=MESH)

    each_remote(lambda step: greet(target(step)))
    for shift in range(1, NY):
        greet(y_target(shift))
    greet(x_target)

    loads[0].wait()
    small = split_matrix(OWN * CTOK * 2)

    def stage_cache(step):
        mixed = cache_raw[:, :, :, columns(step)].reshape(OWN * CTOK * 2, HEAD)
        cache_stage[step] = split_rows(small, mixed).reshape(2, OWN, CTOK, HEAD)

    each(0, SEQ, stage_cache)
    pl.semaphore_wait(barrier, SEQ - 1 + NY)

    per_part = SEQ // PARTS
    for part in range(PARTS):

        def rows_of(step, part=part):
            at = pl.multiple_of((step - part * per_part) * CTOK, CTOK)
            return pools[part].at[0, :, :, pl.ds(at, CTOK), :]

        def send_cache(step, part=part):
            push(cache_stage.at[step], rows_of(step), send_sem.at[0], recv_c.at[part], target(step))

        lo, hi = part * per_part, (part + 1) * per_part
        if lo <= SELF < hi:
            pltpu.make_async_copy(cache_stage.at[SELF], rows_of(SELF), recv_c.at[part]).start()
            each(lo, SELF, send_cache)
            each(SELF + 1, hi, send_cache)
        else:
            each(lo, hi, send_cache)

    loads[1].wait()
    large = split_matrix(TOK * 2)

    def rows(step):
        return pl.ds(pl.multiple_of(step * TOK, TOK), TOK)

    def stage_kv(step):
        mixed = kv_raw[:, :, columns(step)].reshape(TOK * 2, HEAD)
        kv_stage[step] = split_rows(large, mixed).reshape(2, TOK, HEAD)

    def send_kv(step):
        stage_kv(step)
        push(kv_stage.at[step], kv_buf.at[:, rows(step), :], send_sem.at[1], recv_sem.at[1], target(step))

    each_remote(send_kv)
    stage_kv(SELF)
    pltpu.make_async_copy(kv_stage.at[SELF], kv_buf.at[:, rows(SELF), :], recv_sem.at[1]).start()

    loads[2].wait()

    def send_text(step):
        push(text_raw.at[:, :, columns(step)], text_buf.at[seq], send_sem.at[2], recv_sem.at[2], target(step))

    each_remote(send_text)
    pltpu.make_async_copy(text_raw.at[:, :, columns(SELF)], text_buf.at[seq], recv_sem.at[2]).start()

    for part in range(PARTS):
        await_bytes(pools[part].at[0], recv_c.at[part])
        for shift in range(1, NY):
            push(pools[part].at[0], pools[part].at[shift], send_y.at[part], recv_y.at[part], y_target(shift))

    loads[3].wait()

    def send_q(step):
        push(q_raw.at[:, columns(step)], q_buf.at[rows(step), :], send_sem.at[3], recv_q.at[step // 4], target(step))

    each_remote(send_q)
    pltpu.make_async_copy(
        q_raw.at[:, columns(SELF)], q_buf.at[rows(SELF), :], recv_q.at[SELF // 4]
    ).start()

    def entry(clip, w):
        slot = slots[ids[clip, w]]
        owner = slot // OWN
        return owner // NY, (y - owner % NY + NY) % NY, slot % OWN

    partner = (1 - x_hi) * NY + y
    for part in range(PARTS):
        await_bytes(pools[part].at[pl.ds(1, NY - 1)], recv_y.at[part])
        for w in range(WINDOW):
            _, shift, slot = entry(partner, w)
            gives[part][w] = pools[part][shift, :, slot]
        push(gives[part], gots[part], send_x.at[part], recv_x.at[part], x_target)

    for part in range(PARTS):
        await_bytes(gots[part], recv_x.at[part])
        for w in range(WINDOW):
            side, shift, slot = entry(group, w)
            here = jnp.full((2, PART, HEAD), side, jnp.int32) == x_hi
            near = pools[part][shift, :, slot].astype(F32)
            far = gots[part][w].astype(F32)
            window[w, :, part * PART : (part + 1) * PART, :] = jnp.where(here, near, far).astype(BF16)

    await_bytes(text_buf, recv_sem.at[2])
    for half in range(2):
        mixed = text_buf[half * 16 : (half + 1) * 16].reshape(TEXT, HEAD)
        text_kv[:, half * 128 : (half + 1) * 128, :] = split_rows(large, mixed).reshape(2, 128, HEAD)

    await_bytes(kv_buf, recv_sem.at[1])

    live = counts[group]
    biases = [jnp.where(w < live, 0.0, DEAD).astype(F32) for w in range(WINDOW)]
    text_live = lax.broadcasted_iota(jnp.int32, (ROWS, TEXT), 1) < text_counts[group]
    tiles = [(kv_buf.at[0, pl.ds(j * TILE, TILE)], kv_buf.at[1, pl.ds(j * TILE, TILE)], None) for j in range(KEYS // TILE)]
    tiles += [(window.at[w, 0], window.at[w, 1], biases[w]) for w in range(WINDOW)]

    def fold(op, wide):
        part = wide[:, 0:HEAD]
        for u in range(1, wide.shape[1] // HEAD):
            part = op(part, wide[:, u * HEAD : (u + 1) * HEAD])
        return part

    def score(q_rows, keys):
        return lax.dot_general(q_rows, keys, (((1,), (1,)), ((), ())), preferred_element_type=F32)

    ones = jnp.ones((TILE, HEAD), BF16)

    def begin(chunk):
        return q_buf[pl.ds(pl.multiple_of(chunk * ROWS, ROWS), ROWS), :]

    def first_tile(q_rows, side, j, top):
        keys, _, bias = tiles[j]
        s = score(q_rows, keys[...])
        scores[side, :, j * TILE : (j + 1) * TILE] = s
        peak = fold(jnp.maximum, s)
        if bias is not None:
            peak = peak + bias
        return peak if top is None else jnp.maximum(top, peak)

    def first_end(q_rows, side, top):
        s = jnp.where(text_live, score(q_rows, text_kv[0]), DEAD)
        scores[side, :, SPAN : SPAN + TEXT] = s
        text_top = jnp.max(fold(jnp.maximum, s), axis=1, keepdims=True)
        return jnp.max(top, axis=1, keepdims=True), text_top

    def second_tile(side, j, top, mixed):
        _, values, bias = tiles[j]
        shift = top if bias is None else top - bias
        w = jnp.exp2((scores[side, :, j * TILE : (j + 1) * TILE] - shift) * F32(EXP_SCALE))
        both = jnp.concatenate([values[...], ones], axis=1)
        return mixed + jnp.dot(w.astype(BF16), both, preferred_element_type=F32)

    def second_end(chunk, side, text_top, mixed):
        w = jnp.exp2((scores[side, :, SPAN : SPAN + TEXT] - text_top) * F32(EXP_SCALE))
        text_total = jnp.sum(fold(jnp.add, w), axis=1, keepdims=True)
        text_mixed = jnp.dot(w.astype(BF16), text_kv[1], preferred_element_type=F32)
        result = mixed[:, :HEAD] / mixed[:, HEAD:] + text_mixed / text_total
        result = result * F32(SEND_SCALE)
        result = (result * result) * (result * jnp.abs(result))
        o_buf[pl.ds(pl.multiple_of(chunk * ROWS, ROWS), ROWS), :] = result.astype(BF16)

    def advance(chunk, side, tops, follow=True):
        q_rows = begin(chunk + 1) if follow else None
        mixed = jnp.zeros((ROWS, 2 * HEAD), F32)
        top = None
        for j in range(len(tiles)):
            if follow:
                top = first_tile(q_rows, 1 - side, j, top)
            mixed = second_tile(side, j, tops[0], mixed)
        after = first_end(q_rows, 1 - side, top) if follow else None
        second_end(chunk, side, tops[1], mixed)
        return after

    my_columns = pl.ds(pl.multiple_of(head_of(z, x_lo, core) * HEAD, HEAD), HEAD)

    def send_o(step):
        push(o_buf.at[rows(step), :], out_hbm.at[:, my_columns], send_sem.at[4], recv_sem.at[4], target(step, -1))

    def q_ready(chunk):
        await_bytes(q_buf.at[pl.ds(pl.multiple_of(chunk * ROWS, ROWS), ROWS), :], recv_q.at[chunk])

    q_ready(0)
    q_rows = begin(0)
    top = None
    for j in range(len(tiles)):
        top = first_tile(q_rows, 0, j, top)
    tops = first_end(q_rows, 0, top)

    def pair(h, tops):
        for side in range(2):
            chunk = 2 * h + side
            q_ready(chunk + 1)
            tops = advance(chunk, side, tops)
            each(4 * chunk, 4 * chunk + 4, send_o)
        return tops

    tops = lax.fori_loop(0, CHUNKS // 2 - 1, pair, tops)
    q_ready(CHUNKS - 1)
    tops = advance(CHUNKS - 2, 0, tops)
    each(4 * (CHUNKS - 2), 4 * (CHUNKS - 1), send_o)
    advance(CHUNKS - 1, 1, tops, follow=False)
    pltpu.make_async_copy(o_buf.at[rows(SELF), :], out_hbm.at[:, my_columns], recv_sem.at[4]).start()
    each(SELF + 1, SEQ, send_o)

    others = pl.ds(0, SEQ - 1)
    await_bytes(cache_stage.at[others], send_sem.at[0])
    await_bytes(kv_stage.at[others], send_sem.at[1])
    await_bytes(text_buf.at[others], send_sem.at[2])
    await_bytes(q_buf.at[pl.ds(0, (SEQ - 1) * TOK), :], send_sem.at[3])
    for part in range(PARTS):
        await_bytes(pools[part].at[pl.ds(1, NY - 1)], send_y.at[part])
        await_bytes(gives[part], send_x.at[part])
    await_bytes(o_buf.at[pl.ds(0, (SEQ - 1) * TOK), :], send_sem.at[4])
    await_bytes(out_hbm, recv_sem.at[4])


def on_device(queries, current_kv, text_kv, cache_kv, window_ids, window_count, cache_slot, text_count):
    tok, width = queries.shape[1], queries.shape[2]
    hbm = pl.BlockSpec(memory_space=pl.ANY)
    smem = pl.BlockSpec(memory_space=pltpu.SMEM)
    vmem = pltpu.VMEM
    dma = pltpu.SemaphoreType.DMA
    coded = pl.pallas_call(
        body,
        out_shape=jax.ShapeDtypeStruct((tok, width), BF16),
        in_specs=[hbm] * 4 + [smem] * 4,
        out_specs=hbm,
        scratch_shapes=[
            vmem((tok, width), BF16),
            vmem((tok, 2, width), BF16),
            vmem((TTOK, 2, width), BF16),
            vmem((OWN, CTOK, 2, width), BF16),
            vmem((SEQ, 2, TOK, HEAD), BF16),
            vmem((SEQ, 2, OWN, CTOK, HEAD), BF16),
            vmem((KEYS, HEAD), BF16),
            vmem((2, KEYS, HEAD), BF16),
            vmem((SEQ, TTOK, 2, HEAD), BF16),
            vmem((2, TEXT, HEAD), BF16),
        ]
        + [vmem((NY, 2, OWN, PART, HEAD), BF16)] * PARTS
        + [vmem((WINDOW, 2, PART, HEAD), BF16)] * (2 * PARTS)
        + [
            vmem((WINDOW, 2, CACHE, HEAD), BF16),
            vmem((2, ROWS, SPAN + TEXT), F32),
            vmem((KEYS, HEAD), BF16),
            dma((4,)),
            dma((5,)),
            dma((PARTS,)),
            dma((PARTS,)),
            dma((5,)),
            dma((CHUNKS,)),
            dma((PARTS,)),
            dma((PARTS,)),
            dma((PARTS,)),
        ],
        compiler_params=pltpu.CompilerParams(
            collective_id=0, has_side_effects=True, vmem_limit_bytes=58 * 2**20
        ),
        name="attention",
    )(
        queries[0], current_kv[0], text_kv[0], cache_kv,
        window_ids, window_count, cache_slot, text_count,
    )
    coded = coded.astype(F32)
    size = jnp.sqrt(jnp.sqrt(jnp.abs(coded))) * F32(1.0 / SEND_SCALE)
    return jnp.where(coded < 0.0, -size, size).reshape(1, tok, width)


def solution(mesh):
    return jax.shard_map(
        on_device,
        mesh=mesh,
        in_specs=(
            P("group", "seq", None),
            P("group", "seq", None, None),
            P("group", "seq", None, None),
            P("group", "seq", None, None),
            P(),
            P(),
            P(),
            P(),
        ),
        out_specs=P("group", "seq", None),
        check_vma=False,
    )
```

time: 392 us -> 140 us (0.36)
  Pallas kernels: 0 us -> 135 us
  local copies, waits for them, and re-layouts: 94.3 us -> 1.35 us
  waiting for transfers between devices: 88.8 us -> 0 us
  blocking collectives: 55.5 us -> 0 us
  other arithmetic: 56.9 us -> 3.9 us
  matrix products: 47.7 us -> 0 us
  starting transfers between devices: 33.6 us -> 0 us
  between operations: 13.6 us -> 0.01 us
    pallas_call x0 -> x1, Pallas kernels: none -> 135 us  [on_device(): pl.pallas_call(body, out_shape=jax.ShapeDtypeStruct((tok, width), BF16),...]
    all_gather x1 -> x0, waiting for transfers between devices: 59 us -> none  [on_device(): pool_rows = lax.all_gather(cache_kv, 'group', axis=0, tiled=True)]
    all_to_all x1 -> x0, blocking collectives: 55.5 us -> none  [on_device(): lax.all_to_all(merged, 'seq', split_axis=0, concat_axis=1, tiled=True)]
    dot_general x32 -> x0, matrix products: 47.7 us -> none  [the longest x16 28.6 us: attend(): jnp.dot(weights.astype(jnp.bfloat16), value_rows, preferred_element_type=...]
    unnamed x36 -> x1, local copies, waits for them, and re-layouts: 47.2 us -> 1.35 us
    all_to_all x4 -> x0, starting transfers between devices: 33.6 us -> none  [the longest x1 11 us: on_device(): lax.all_to_all(text_cols, 'seq', split_axis=2, concat_axis=0, tiled=True)]
    all_to_all x4 -> x0, waiting for transfers between devices: 29.8 us -> none  [the longest x1 22.5 us: on_device(): lax.all_to_all(query_cols, 'seq', split_axis=2, concat_axis=0, tiled=True)]
    reduce_sum x16 -> x0, other arithmetic: 23.9 us -> none  [attend(): row_sum = jnp.sum(weights, axis=1, keepdims=True)]
  transfers between devices with their start and end apart: 5 -> 0, of which waited for: 3 -> 0; matrix products, arithmetic and copies ran while one was open for 23% -> 0% of each run, Pallas kernels for 0% -> 0%
where the time goes in v1:
time: 140 us
  Pallas kernels  135 us (96%)
  other arithmetic  3.9 us (3%)
    pallas_call x1, Pallas kernels, on_device(): pl.pallas_call(body, out_shape=jax.ShapeDtypeStruct((tok, width), BF16),...  135 us
    reshape x1, other arithmetic, on_device(): return jnp.where(coded < 0.0, -size, size).reshape(1, tok, width)  3.9 us

profile of v1, /device:TPU:1, one launch (start us, length us, event | category | flops | bytes accessed | tf_op | source)
XLA Modules:
  0.0 139.8 jit_solution(14556988214898627238)
XLA Ops:
  0.0 1.3 copy.9.ids
  1.3 134.6 %attention.1 = bf16[128,4096]{1,0:T(8,128)(2,1)} custom-call(bf16[128,4096]{1,0:T(8,128)(2,1)} %bitcast.6, bf16[128,2,4096]{2,1,0:T(2,128)(2,1)} %bitcast.5, bf16[8,2,4096]{2,1,0:T(2,128)(2,1)} %bitcast.7, bf16[4,16,2,4096]{3,2,1,0:T(2,128)(2,1)} %cache_hbm.1, s32[8,4]{1,0:T(8,128)} %copy.9.ids, s32[8]{0:T(128)} %counts.1, s32[32]{0:T(128)} %slots.1, ...), custom_call_target="tpu_custom_call" | custom-call | tf_op jit(solution)/shard_map/attention/pallas_call | solution.py:335
  135.9 3.9 %fusion.3 = f32[1,128,4096]{2,1,0:T(8,128)} fusion(bf16[128,4096]{1,0:T(8,128)(2,1)} %attention.1), kind=kLoop, calls=%fused_computation.6 | loop fusion | flops 3145728 | bytes 3145728 | tf_op jit(solution)/shard_map/reshape | solution.py:378

commit v2 on v1

--- a/solution.py
+++ b/solution.py
@@ -68,9 +68,12 @@
         return z_at * 4 + ((x_at + x_hi) % 2) * 2 + core_at
 
     def place(step, sign):
-        n = (step // 4 + 1) % NZ
-        shift = (2 * (n % 2) - 1) * ((n + 1) // 2) * sign
-        return (z + shift + NZ) % NZ, (x_lo + (step % 4) // 2) % 2, (core + step % 2) % 2
+        i, q = step // 4, step % 4
+        both = (i % 7 + 6) // 7
+        planes = 4 - (i + 1) // 2
+        shift = (1 - 2 * (q // 2) * both) * planes * sign
+        dx = both * ((i + 1) % 2) + (1 - both) * (q // 2)
+        return (z + shift + NZ) % NZ, (x_lo + dx) % 2, (core + q % 2) % 2
 
     def target(step, sign=1):
         z_at, x_at, core_at = place(step, sign)
@@ -109,8 +112,8 @@
             ((cache_hbm, cache_raw), (kv_hbm, kv_raw), (text_hbm, text_raw), (q_hbm, q_raw))
         )
     ]
-    for load in loads:
-        load.start()
+    for i in (3, 0, 1, 2):
+        loads[i].start()
 
     barrier = pltpu.get_barrier_semaphore()
 
@@ -122,6 +125,17 @@
         greet(y_target(shift))
     greet(x_target)
 
+    pl.semaphore_wait(barrier, SEQ - 1 + NY)
+
+    def rows(step):
+        return pl.ds(pl.multiple_of(step * TOK, TOK), TOK)
+
+    def send_q(step):
+        push(q_raw.at[:, columns(step)], q_buf.at[rows(step), :], send_sem.at[3], recv_q.at[step // 4], target(step))
+
+    loads[3].wait()
+    each(0, 4, send_q)
+
     loads[0].wait()
     small = split_matrix(OWN * CTOK * 2)
 
@@ -129,9 +143,6 @@
         mixed = cache_raw[:, :, :, columns(step)].reshape(OWN * CTOK * 2, HEAD)
         cache_stage[step] = split_rows(small, mixed).reshape(2, OWN, CTOK, HEAD)
 
-    each(0, SEQ, stage_cache)
-    pl.semaphore_wait(barrier, SEQ - 1 + NY)
-
     per_part = SEQ // PARTS
     for part in range(PARTS):
 
@@ -140,10 +151,12 @@
             return pools[part].at[0, :, :, pl.ds(at, CTOK), :]
 
         def send_cache(step, part=part):
+            stage_cache(step)
             push(cache_stage.at[step], rows_of(step), send_sem.at[0], recv_c.at[part], target(step))
 
         lo, hi = part * per_part, (part + 1) * per_part
         if lo <= SELF < hi:
+            stage_cache(SELF)
             pltpu.make_async_copy(cache_stage.at[SELF], rows_of(SELF), recv_c.at[part]).start()
             each(lo, SELF, send_cache)
             each(SELF + 1, hi, send_cache)
@@ -153,9 +166,6 @@
     loads[1].wait()
     large = split_matrix(TOK * 2)
 
-    def rows(step):
-        return pl.ds(pl.multiple_of(step * TOK, TOK), TOK)
-
     def stage_kv(step):
         mixed = kv_raw[:, :, columns(step)].reshape(TOK * 2, HEAD)
         kv_stage[step] = split_rows(large, mixed).reshape(2, TOK, HEAD)
@@ -181,18 +191,14 @@
         for shift in range(1, NY):
             push(pools[part].at[0], pools[part].at[shift], send_y.at[part], recv_y.at[part], y_target(shift))
 
-    loads[3].wait()
-
-    def send_q(step):
-        push(q_raw.at[:, columns(step)], q_buf.at[rows(step), :], send_sem.at[3], recv_q.at[step // 4], target(step))
-
-    each_remote(send_q)
+    each(4, SELF, send_q)
+    each(SELF + 1, SEQ, send_q)
     pltpu.make_async_copy(
         q_raw.at[:, columns(SELF)], q_buf.at[rows(SELF), :], recv_q.at[SELF // 4]
     ).start()
 
     def entry(clip, w):
-        slot = slots[ids[clip, w]]
+        slot = slots[ids[w, clip]]
         owner = slot // OWN
         return owner // NY, (y - owner % NY + NY) % NY, slot % OWN
 
@@ -371,10 +377,10 @@
         name="attention",
     )(
         queries[0], current_kv[0], text_kv[0], cache_kv,
-        window_ids, window_count, cache_slot, text_count,
+        window_ids.T, window_count, cache_slot, text_count,
     )
     coded = coded.astype(F32)
-    size = jnp.sqrt(jnp.sqrt(jnp.abs(coded))) * F32(1.0 / SEND_SCALE)
+    size = lax.rsqrt(lax.rsqrt(jnp.abs(coded))) * F32(1.0 / SEND_SCALE)
     return jnp.where(coded < 0.0, -size, size).reshape(1, tok, width)
 
 

time: 140 us -> 136 us (0.971)
  Pallas kernels: 135 us -> 133 us
    pallas_call x1, Pallas kernels: 135 us -> 133 us  [on_device(): pl.pallas_call(body, out_shape=jax.ShapeDtypeStruct((tok, width), BF16),...]
where the time goes in v2:
time: 136 us
  Pallas kernels  133 us (98%)
  other arithmetic  3.1 us (2%)
    pallas_call x1, Pallas kernels, on_device(): pl.pallas_call(body, out_shape=jax.ShapeDtypeStruct((tok, width), BF16),...  133 us
    reshape x1, other arithmetic, on_device(): return jnp.where(coded < 0.0, -size, size).reshape(1, tok, width)  3.1 us

profile of v2, /device:TPU:1, one launch (start us, length us, event | category | flops | bytes accessed | tf_op | source)
XLA Modules:
  0.0 136.0 jit_solution(17047155450582598520)
XLA Ops:
  0.0 132.9 %attention.1 = bf16[128,4096]{1,0:T(8,128)(2,1)} custom-call(bf16[128,4096]{1,0:T(8,128)(2,1)} %bitcast.7, bf16[128,2,4096]{2,1,0:T(2,128)(2,1)} %bitcast.6, bf16[8,2,4096]{2,1,0:T(2,128)(2,1)} %bitcast.8, bf16[4,16,2,4096]{3,2,1,0:T(2,128)(2,1)} %cache_hbm.1, s32[4,8]{1,0:T(4,128)} %bitcast.9, s32[8]{0:T(128)} %counts.1, s32[32]{0:T(128)} %slots.1, ...), custom_call_target="tpu_custom_call" | custom-call | tf_op jit(solution)/shard_map/attention/pallas_call | solution.py:341
  132.9 3.1 %fusion.3 = f32[1,128,4096]{2,1,0:T(8,128)} fusion(bf16[128,4096]{1,0:T(8,128)(2,1)} %attention.1), kind=kLoop, calls=%fused_computation.6 | loop fusion | flops 3145728 | bytes 3145728 | tf_op jit(solution)/shard_map/reshape | solution.py:384

commit v3 on v2

--- a/solution.py
+++ b/solution.py
@@ -24,7 +24,7 @@
 SPAN = KEYS + WINDOW * CACHE
 PARTS = 4
 PART = CACHE // PARTS
-SELF = 28
+SELF = 4
 DEAD = -1e30
 EXP_SCALE = math.log2(math.e) / math.sqrt(HEAD)
 SEND_SCALE = 2.0**28
@@ -54,7 +54,7 @@
     give_0, give_1, give_2, give_3,
     got_0, got_1, got_2, got_3,
     window, scores, o_buf,
-    load_sem, send_sem, send_y, send_x, recv_sem, recv_q, recv_c, recv_y, recv_x,
+    load_sem, send_sem, send_y, send_x, recv_sem, recv_kv, recv_q, recv_c, recv_y, recv_x,
 ):
     pools = (pool_0, pool_1, pool_2, pool_3)
     gives = (give_0, give_1, give_2, give_3)
@@ -68,7 +68,7 @@
         return z_at * 4 + ((x_at + x_hi) % 2) * 2 + core_at
 
     def place(step, sign):
-        i, q = step // 4, step % 4
+        i, q = (step // 4 + 6) % 8, step % 4
         both = (i % 7 + 6) // 7
         planes = 4 - (i + 1) // 2
         shift = (1 - 2 * (q // 2) * both) * planes * sign
@@ -134,7 +134,11 @@
         push(q_raw.at[:, columns(step)], q_buf.at[rows(step), :], send_sem.at[3], recv_q.at[step // 4], target(step))
 
     loads[3].wait()
-    each(0, 4, send_q)
+    each(0, SELF, send_q)
+    each(SELF + 1, 8, send_q)
+    pltpu.make_async_copy(
+        q_raw.at[:, columns(SELF)], q_buf.at[rows(SELF), :], recv_q.at[SELF // 4]
+    ).start()
 
     loads[0].wait()
     small = split_matrix(OWN * CTOK * 2)
@@ -163,6 +167,14 @@
         else:
             each(lo, hi, send_cache)
 
+    loads[2].wait()
+
+    def send_text(step):
+        push(text_raw.at[:, :, columns(step)], text_buf.at[seq], send_sem.at[2], recv_sem.at[2], target(step))
+
+    each_remote(send_text)
+    pltpu.make_async_copy(text_raw.at[:, :, columns(SELF)], text_buf.at[seq], recv_sem.at[2]).start()
+
     loads[1].wait()
     large = split_matrix(TOK * 2)
 
@@ -170,32 +182,27 @@
         mixed = kv_raw[:, :, columns(step)].reshape(TOK * 2, HEAD)
         kv_stage[step] = split_rows(large, mixed).reshape(2, TOK, HEAD)
 
-    def send_kv(step):
+    def send_kv(step, kind):
+        push(kv_stage.at[step, kind], kv_buf.at[kind, rows(step), :], send_sem.at[1], recv_kv.at[kind], target(step))
+
+    def send_keys(step):
         stage_kv(step)
-        push(kv_stage.at[step], kv_buf.at[:, rows(step), :], send_sem.at[1], recv_sem.at[1], target(step))
-
-    each_remote(send_kv)
+        send_kv(step, 0)
+
+    each_remote(send_keys)
     stage_kv(SELF)
-    pltpu.make_async_copy(kv_stage.at[SELF], kv_buf.at[:, rows(SELF), :], recv_sem.at[1]).start()
-
-    loads[2].wait()
-
-    def send_text(step):
-        push(text_raw.at[:, :, columns(step)], text_buf.at[seq], send_sem.at[2], recv_sem.at[2], target(step))
-
-    each_remote(send_text)
-    pltpu.make_async_copy(text_raw.at[:, :, columns(SELF)], text_buf.at[seq], recv_sem.at[2]).start()
+    for kind in range(2):
+        pltpu.make_async_copy(
+            kv_stage.at[SELF, kind], kv_buf.at[kind, rows(SELF), :], recv_kv.at[kind]
+        ).start()
+    each_remote(lambda step: send_kv(step, 1))
 
     for part in range(PARTS):
         await_bytes(pools[part].at[0], recv_c.at[part])
         for shift in range(1, NY):
             push(pools[part].at[0], pools[part].at[shift], send_y.at[part], recv_y.at[part], y_target(shift))
 
-    each(4, SELF, send_q)
-    each(SELF + 1, SEQ, send_q)
-    pltpu.make_async_copy(
-        q_raw.at[:, columns(SELF)], q_buf.at[rows(SELF), :], recv_q.at[SELF // 4]
-    ).start()
+    each(8, SEQ, send_q)
 
     def entry(clip, w):
         slot = slots[ids[w, clip]]
@@ -224,7 +231,7 @@
         mixed = text_buf[half * 16 : (half + 1) * 16].reshape(TEXT, HEAD)
         text_kv[:, half * 128 : (half + 1) * 128, :] = split_rows(large, mixed).reshape(2, 128, HEAD)
 
-    await_bytes(kv_buf, recv_sem.at[1])
+    await_bytes(kv_buf.at[0], recv_kv.at[0])
 
     live = counts[group]
     biases = [jnp.where(w < live, 0.0, DEAD).astype(F32) for w in range(WINDOW)]
@@ -304,21 +311,29 @@
         top = first_tile(q_rows, 0, j, top)
     tops = first_end(q_rows, 0, top)
 
+    def send_chunk(chunk):
+        own = jnp.where(chunk == SELF // 4, 1, 0)
+        each(4 * chunk + own, 4 * chunk + 4, send_o)
+
+        @pl.when(chunk == SELF // 4)
+        def _():
+            pltpu.make_async_copy(o_buf.at[rows(SELF), :], out_hbm.at[:, my_columns], recv_sem.at[4]).start()
+
     def pair(h, tops):
         for side in range(2):
             chunk = 2 * h + side
             q_ready(chunk + 1)
             tops = advance(chunk, side, tops)
-            each(4 * chunk, 4 * chunk + 4, send_o)
+            send_chunk(chunk)
         return tops
 
+    await_bytes(kv_buf.at[1], recv_kv.at[1])
     tops = lax.fori_loop(0, CHUNKS // 2 - 1, pair, tops)
     q_ready(CHUNKS - 1)
     tops = advance(CHUNKS - 2, 0, tops)
     each(4 * (CHUNKS - 2), 4 * (CHUNKS - 1), send_o)
     advance(CHUNKS - 1, 1, tops, follow=False)
-    pltpu.make_async_copy(o_buf.at[rows(SELF), :], out_hbm.at[:, my_columns], recv_sem.at[4]).start()
-    each(SELF + 1, SEQ, send_o)
+    each(4 * (CHUNKS - 1), SEQ, send_o)
 
     others = pl.ds(0, SEQ - 1)
     await_bytes(cache_stage.at[others], send_sem.at[0])
@@ -366,6 +381,7 @@
             dma((PARTS,)),
             dma((PARTS,)),
             dma((5,)),
+            dma((2,)),
             dma((CHUNKS,)),
             dma((PARTS,)),
             dma((PARTS,)),

time: 136 us -> 133 us (0.978)
  Pallas kernels: 133 us -> 130 us
    pallas_call x1, Pallas kernels: 133 us -> 130 us  [on_device(): pl.pallas_call(body, out_shape=jax.ShapeDtypeStruct((tok, width), BF16),...]
where the time goes in v3:
time: 133 us
  Pallas kernels  130 us (98%)
  other arithmetic  3.1 us (2%)
    pallas_call x1, Pallas kernels, on_device(): pl.pallas_call(body, out_shape=jax.ShapeDtypeStruct((tok, width), BF16),...  130 us
    reshape x1, other arithmetic, on_device(): return jnp.where(coded < 0.0, -size, size).reshape(1, tok, width)  3.1 us

profile of v3, /device:TPU:1, one launch (start us, length us, event | category | flops | bytes accessed | tf_op | source)
XLA Modules:
  0.0 133.2 jit_solution(9114212795286552127)
XLA Ops:
  0.0 130.1 %attention.1 = bf16[128,4096]{1,0:T(8,128)(2,1)} custom-call(bf16[128,4096]{1,0:T(8,128)(2,1)} %bitcast.7, bf16[128,2,4096]{2,1,0:T(2,128)(2,1)} %bitcast.6, bf16[8,2,4096]{2,1,0:T(2,128)(2,1)} %bitcast.8, bf16[4,16,2,4096]{3,2,1,0:T(2,128)(2,1)} %cache_hbm.1, s32[4,8]{1,0:T(4,128)} %bitcast.9, s32[8]{0:T(128)} %counts.1, s32[32]{0:T(128)} %slots.1, ...), custom_call_target="tpu_custom_call" | custom-call | tf_op jit(solution)/shard_map/attention/pallas_call | solution.py:356
  130.1 3.1 %fusion.3 = f32[1,128,4096]{2,1,0:T(8,128)} fusion(bf16[128,4096]{1,0:T(8,128)(2,1)} %attention.1), kind=kLoop, calls=%fused_computation.6 | loop fusion | flops 3145728 | bytes 3145728 | tf_op jit(solution)/shard_map/reshape | solution.py:400

commit v4 on v3

--- a/solution.py
+++ b/solution.py
@@ -25,6 +25,8 @@
 PARTS = 4
 PART = CACHE // PARTS
 SELF = 4
+PIECES = 4
+PIECE = TOK // PIECES
 DEAD = -1e30
 EXP_SCALE = math.log2(math.e) / math.sqrt(HEAD)
 SEND_SCALE = 2.0**28
@@ -345,6 +347,25 @@
         await_bytes(gives[part], send_x.at[part])
     await_bytes(o_buf.at[pl.ds(0, (SEQ - 1) * TOK), :], send_sem.at[4])
     await_bytes(out_hbm, recv_sem.at[4])
+
+
+def decode(coded_hbm, out_hbm, coded, out, load_sem, store_sem):
+    loads, stores = [], []
+    for i in range(PIECES):
+        at = pl.ds(i * PIECE, PIECE)
+        loads.append(pltpu.make_async_copy(coded_hbm.at[at], coded.at[i], load_sem.at[i]))
+        stores.append(pltpu.make_async_copy(out.at[i], out_hbm.at[at], store_sem.at[i]))
+    for load in loads:
+        load.start()
+    for i in range(PIECES):
+        loads[i].wait()
+        power = coded[i].astype(F32)
+        size = lax.rsqrt(lax.rsqrt(jnp.abs(power))) * F32(1.0 / SEND_SCALE)
+        size = jnp.where(power == 0.0, 0.0, size)
+        out[i] = jnp.where(power < 0.0, -size, size)
+        stores[i].start()
+    for store in stores:
+        store.wait()
 
 
 def on_device(queries, current_kv, text_kv, cache_kv, window_ids, window_count, cache_slot, text_count):
@@ -395,9 +416,20 @@
         queries[0], current_kv[0], text_kv[0], cache_kv,
         window_ids.T, window_count, cache_slot, text_count,
     )
-    coded = coded.astype(F32)
-    size = lax.rsqrt(lax.rsqrt(jnp.abs(coded))) * F32(1.0 / SEND_SCALE)
-    return jnp.where(coded < 0.0, -size, size).reshape(1, tok, width)
+    return pl.pallas_call(
+        decode,
+        out_shape=jax.ShapeDtypeStruct((tok, width), F32),
+        in_specs=[hbm],
+        out_specs=hbm,
+        scratch_shapes=[
+            vmem((PIECES, PIECE, width), BF16),
+            vmem((PIECES, PIECE, width), F32),
+            dma((PIECES,)),
+            dma((PIECES,)),
+        ],
+        compiler_params=pltpu.CompilerParams(vmem_limit_bytes=58 * 2**20),
+        name="decode",
+    )(coded).reshape(1, tok, width)
 
 
 def solution(mesh):

time: 133 us -> 133 us (level)
  other arithmetic: 3.1 us -> 0 us
  Pallas kernels: 130 us -> 133 us
    reshape x1 -> x0, other arithmetic: 3.1 us -> none  [on_device(): return jnp.where(coded < 0.0, -size, size).reshape(1, tok, width)]
    pallas_call x0 -> x1, Pallas kernels: none -> 2.54 us  [on_device(): pl.pallas_call(decode, out_shape=jax.ShapeDtypeStruct((tok, width), F32),...]
where the time goes in v4:
time: 133 us
  Pallas kernels  133 us (100%)
    pallas_call x1, Pallas kernels, on_device(): pl.pallas_call(body, out_shape=jax.ShapeDtypeStruct((tok, width), BF16),...  130 us

profile of v4, /device:TPU:1, one launch (start us, length us, event | category | flops | bytes accessed | tf_op | source)
XLA Modules:
  0.0 132.8 jit_solution(43559942671472817)
XLA Ops:
  0.0 130.1 %attention.1.coded_hbm = bf16[128,4096]{1,0:T(8,128)(2,1)} custom-call(bf16[128,4096]{1,0:T(8,128)(2,1)} %bitcast.6, bf16[128,2,4096]{2,1,0:T(2,128)(2,1)} %bitcast.5, bf16[8,2,4096]{2,1,0:T(2,128)(2,1)} %bitcast.7, bf16[4,16,2,4096]{3,2,1,0:T(2,128)(2,1)} %cache_hbm.1, s32[4,8]{1,0:T(4,128)} %bitcast.8, s32[8]{0:T(128)} %counts.1, s32[32]{0:T(128)} %slots.1, ...), custom_call_target="tpu_custom_call" | custom-call | tf_op jit(solution)/shard_map/attention/pallas_call | solution.py:377
  130.1 2.5 %decode.1 = f32[128,4096]{1,0:T(8,128)} custom-call(bf16[128,4096]{1,0:T(8,128)(2,1)} %attention.1.coded_hbm), custom_call_target="tpu_custom_call" | custom-call | tf_op jit(solution)/shard_map/decode/pallas_call | solution.py:419
